TPU v7x, 32 devices: a whole 2x2x4 slice. The times are simulated.
32 devices in a mesh: seq: 16 (over z, y, core), hd: 2 (over x).
Axes of the slice: x: 2, y: 2, z: 4, core: 2. Of those that a mesh axis runs over, the one named last changes fastest.
Arguments:
- tokens: bfloat16 [24576, 768], P(('seq', 'hd')), may hold values from -6 to 6
- image_ids: int32 [24576], P(('seq', 'hd')), may hold values from 0 to 11, as said below
- keep_masks: int32 [16, 12, 2], P('seq'), may hold values 0 or 1
- ln1_gain: float32 [768], replicated, may hold values from 0.5 to 1.5
- ln1_bias: float32 [768], replicated, may hold values from -4 to 4
- w_qkv: bfloat16 [768, 2304], replicated, may hold values from -0.21875 to 0.21875
- qv_bias: float32 [1536], replicated, may hold values from -6 to 6
- w_out: bfloat16 [768, 768], replicated, may hold values from -0.875 to 0.875
- b_out: float32 [768], replicated, may hold values from -4 to 4
- ln2_gain: float32 [768], replicated, may hold values from 0.5 to 1.5
- ln2_bias: float32 [768], replicated, may hold values from -4 to 4
- w_fc1: bfloat16 [768, 3072], replicated, may hold values from -0.21875 to 0.21875
- b_fc1: float32 [3072], replicated, may hold values from -6 to 6
- w_fc2: bfloat16 [3072, 768], replicated, may hold values from -0.109375 to 0.109375
- b_fc2: float32 [768], replicated, may hold values from -4 to 4
- cotangent: bfloat16 [24576, 768], P(('seq', 'hd')), may hold values from -6 to 6
Outputs:
- mixed: bfloat16 [24576, 768], P(('seq', 'hd'))
- grad_tokens: float32 [24576, 768], P(('seq', 'hd'))
- grad_ln1_gain: float32 [768], P(('seq', 'hd'))
- grad_ln1_bias: float32 [768], P(('seq', 'hd'))
- grad_w_qkv: float32 [768, 2304], P(('seq', 'hd'))
- grad_qv_bias: float32 [1536], P(('seq', 'hd'))
- grad_w_out: float32 [768, 768], P(('seq', 'hd'))
- grad_b_out: float32 [768], P(('seq', 'hd'))
- grad_ln2_gain: float32 [768], P(('seq', 'hd'))
- grad_ln2_bias: float32 [768], P(('seq', 'hd'))
- grad_w_fc1: float32 [768, 3072], P(('seq', 'hd'))
- grad_b_fc1: float32 [3072], P(('seq', 'hd'))
- grad_w_fc2: float32 [3072, 768], P(('seq', 'hd'))
- grad_b_fc2: float32 [768], P(('seq', 'hd'))
Inputs may be any that keep to these rules, and one draw needn't show every extreme that they name: `image_ids`: within each pack of 1536 rows the image number starts at 0 and rises by one from image to image; images are runs of 102, 198 or 578 rows, except that the image just before a 578-row image and the pack's last image may be cut short; a 578-row image covers rows 767 and 768 of every pack.
All inputs are finite; a program needn't handle non-finite values. No bound on the sum of `keep_masks` on one device may be relied on, other than what follows from the above.
Results may differ from a plain program's by a relative error of at most 0.0095.
Values may be sent and summed in bfloat16 or wider, within the bound.
A program may use at most 192 MiB of HBM per device.

v0:
```python
import jax
import jax.numpy as jnp
from jax import lax
from jax.sharding import PartitionSpec as P

HEADS = 12
HEAD = 64


ln_epsilon = 1e-06
drop_scale = 1.0 / 0.9
masked_score = -1e30


def layer_norm(values, gain_row, bias_row):
    center = values - jnp.mean(values, -1, keepdims=True)
    variance = jnp.mean(center * center, -1, keepdims=True)
    return center * lax.rsqrt(variance + ln_epsilon) * gain_row + bias_row


def gelu_exact(values):
    return jax.nn.gelu(values, approximate=False)


def left_product(left_side, right_side):
    return lax.dot_general(
        left_side, right_side, (((0,), (0,)), ((), ())), preferred_element_type=jnp.float32
    )


def right_product(left_side, right_side):
    return lax.dot_general(
        left_side, right_side, (((1,), (1,)), ((), ())), preferred_element_type=jnp.float32
    )


def pick_block(total_rows):
    for candidate in (512, 768, 1024):
        return candidate
    return total_rows


def block_scores(query_rows, owner_rows, keys_all, key_owners, score_scale):
    scores = (
        jnp.einsum("qhd,khd->hqk", query_rows, keys_all, preferred_element_type=jnp.float32)
        * score_scale
    )
    same_image = owner_rows[:, None] == key_owners[None, :]
    return jnp.where(same_image[None], scores, masked_score)


def attend_forward(queries, query_owners, keys_all, values_all, key_owners, score_scale):
    query_count = queries.shape[0]
    block_rows = pick_block(query_count)
    block_count = query_count // block_rows

    def one_block(block_index):
        first_row = block_index * block_rows
        query_rows = lax.dynamic_slice_in_dim(queries, first_row, block_rows, 0)
        owner_rows = lax.dynamic_slice_in_dim(query_owners, first_row, block_rows, 0)
        scores = block_scores(query_rows, owner_rows, keys_all, key_owners, score_scale)
        row_peak = jnp.max(scores, -1, keepdims=True)
        weights = jnp.exp(scores - row_peak)
        row_total = jnp.sum(weights, -1, keepdims=True)
        prob_low = (weights / row_total).astype(jnp.bfloat16)
        block_out = jnp.einsum(
            "hqk,khd->qhd", prob_low, values_all, preferred_element_type=jnp.float32
        )
        return (block_out, (row_peak + jnp.log(row_total))[..., 0])

    block_outs, log_totals = lax.map(one_block, jnp.arange(block_count))
    return (block_outs.reshape(query_count, queries.shape[1], queries.shape[2]), log_totals)


def attend_backward(
    queries, query_owners, keys_all, values_all, key_owners, log_totals, grad_out, score_scale
):
    query_count = queries.shape[0]
    block_rows = pick_block(query_count)
    block_count = query_count // block_rows

    def one_block(running, block_index):
        grad_keys, grad_values = running
        first_row = block_index * block_rows
        query_rows = lax.dynamic_slice_in_dim(queries, first_row, block_rows, 0)
        owner_rows = lax.dynamic_slice_in_dim(query_owners, first_row, block_rows, 0)
        grad_rows = lax.dynamic_slice_in_dim(grad_out, first_row, block_rows, 0)
        scores = block_scores(query_rows, owner_rows, keys_all, key_owners, score_scale)
        prob_full = jnp.exp(scores - log_totals[block_index][..., None])
        prob_low = prob_full.astype(jnp.bfloat16)
        grad_probs = jnp.einsum(
            "qhd,khd->hqk", grad_rows, values_all, preferred_element_type=jnp.float32
        )
        grad_scores = prob_full * (grad_probs - jnp.sum(prob_full * grad_probs, -1, keepdims=True))
        grad_low = grad_scores.astype(jnp.bfloat16)
        grad_query = (
            jnp.einsum("hqk,khd->qhd", grad_low, keys_all, preferred_element_type=jnp.float32)
            * score_scale
        )
        grad_keys = (
            grad_keys
            + jnp.einsum("hqk,qhd->khd", grad_low, query_rows, preferred_element_type=jnp.float32)
            * score_scale
        )
        grad_values = grad_values + jnp.einsum(
            "hqk,qhd->khd", prob_low, grad_rows, preferred_element_type=jnp.float32
        )
        return ((grad_keys, grad_values), grad_query)

    zero_grads = jnp.zeros(keys_all.shape, jnp.float32)
    (grad_keys, grad_values), grad_queries = lax.scan(
        one_block, (zero_grads, zero_grads), jnp.arange(block_count)
    )
    return (grad_queries.reshape(queries.shape), grad_keys, grad_values)


def per_device(
    tokens,
    image_ids,
    keep_masks,
    ln1_gain,
    ln1_bias,
    w_qkv,
    qv_bias,
    w_out,
    b_out,
    ln2_gain,
    ln2_bias,
    w_fc1,
    b_fc1,
    w_fc2,
    b_fc2,
    cotangent,
):
    tok_rows, model_width = tokens.shape
    pair_count = lax.axis_size("hd")
    heads_here = HEADS // pair_count
    head_width = heads_here * HEAD
    score_scale = HEAD ** (-0.5)
    group_rows = tok_rows * pair_count
    inputs = tokens.astype(jnp.float32)
    slot_count = keep_masks.shape[1]
    one_hot = (image_ids[:, None] == jnp.arange(slot_count, dtype=jnp.int32)[None, :]).astype(
        jnp.float32
    )
    keep_rows = jnp.dot(one_hot, keep_masks[0].astype(jnp.float32)) * drop_scale
    normed_first = layer_norm(inputs, ln1_gain, ln1_bias).astype(jnp.bfloat16)
    bias_all = jnp.concatenate(
        [qv_bias[:model_width], jnp.zeros((model_width,), jnp.float32), qv_bias[model_width:]]
    )
    projected = (
        jnp.dot(normed_first, w_qkv, preferred_element_type=jnp.float32) + bias_all
    ).astype(jnp.bfloat16)
    owner_local = jnp.broadcast_to(
        image_ids.astype(jnp.bfloat16)[:, None, None, None], (tok_rows, 1, pair_count, 1)
    )
    grouped, owners = (
        lax.all_to_all(
            projected.reshape(tok_rows, 3, pair_count, head_width),
            "hd",
            split_axis=2,
            concat_axis=0,
            tiled=True,
        ),
        lax.all_to_all(owner_local, "hd", split_axis=2, concat_axis=0, tiled=True),
    )
    owners = owners.reshape(group_rows)
    grouped = grouped.reshape(group_rows, 3, heads_here, HEAD)
    queries = grouped[:, 0]
    keys_all = grouped[:, 1]
    values_all = grouped[:, 2]
    attended, log_totals = attend_forward(
        queries, owners, keys_all, values_all, owners, score_scale
    )
    attended_low = attended.reshape(group_rows, 1, head_width).astype(jnp.bfloat16)
    gathered_heads = lax.all_to_all(
        attended_low, "hd", split_axis=0, concat_axis=1, tiled=True
    ).reshape(tok_rows, model_width)
    branch = jnp.dot(gathered_heads, w_out, preferred_element_type=jnp.float32) + b_out
    middle = inputs + keep_rows[:, 0:1] * branch
    normed_second = layer_norm(middle, ln2_gain, ln2_bias).astype(jnp.bfloat16)
    hidden_pre = jnp.dot(normed_second, w_fc1, preferred_element_type=jnp.float32) + b_fc1
    activated, gelu_pull = jax.vjp(gelu_exact, hidden_pre)
    activated_low = activated.astype(jnp.bfloat16)
    mlp_out = jnp.dot(activated_low, w_fc2, preferred_element_type=jnp.float32) + b_fc2
    mixed_out = (middle + keep_rows[:, 1:2] * mlp_out).astype(jnp.bfloat16)
    grad_result = cotangent.astype(jnp.float32)
    grad_mlp = (grad_result * keep_rows[:, 1:2]).astype(jnp.bfloat16)
    grad_b_fc2 = jnp.sum(grad_mlp.astype(jnp.float32), 0)
    grad_w_fc2 = left_product(activated_low, grad_mlp)
    grad_act = right_product(grad_mlp, w_fc2)
    grad_hidden = gelu_pull(grad_act)[0].astype(jnp.bfloat16)
    grad_b_fc1 = jnp.sum(grad_hidden.astype(jnp.float32), 0)
    grad_w_fc1 = left_product(normed_second, grad_hidden)
    grad_normed_second = right_product(grad_hidden, w_fc1)
    second_pull = jax.vjp(layer_norm, middle, ln2_gain, ln2_bias)[1]
    grad_mid_norm, grad_ln2_gain, grad_ln2_bias = second_pull(grad_normed_second)
    grad_middle = grad_result + grad_mid_norm
    grad_branch = (grad_middle * keep_rows[:, 0:1]).astype(jnp.bfloat16)
    grad_b_out = jnp.sum(grad_branch.astype(jnp.float32), 0)
    grad_w_out = left_product(gathered_heads, grad_branch)
    grad_heads = right_product(grad_branch, w_out).astype(jnp.bfloat16)
    grad_attended = lax.all_to_all(
        grad_heads.reshape(tok_rows, pair_count, head_width),
        "hd",
        split_axis=1,
        concat_axis=0,
        tiled=True,
    ).reshape(group_rows, heads_here, HEAD)
    grad_queries, grad_keys, grad_values = attend_backward(
        queries, owners, keys_all, values_all, owners, log_totals, grad_attended, score_scale
    )
    stacked = jnp.stack([grad_queries, grad_keys, grad_values], 1).astype(jnp.bfloat16)
    grad_projected = lax.all_to_all(
        stacked.reshape(group_rows, 3, 1, head_width), "hd", split_axis=0, concat_axis=2, tiled=True
    ).reshape(tok_rows, 3 * model_width)
    column_sums = jnp.sum(grad_projected.astype(jnp.float32), 0)
    grad_qv_bias = jnp.concatenate([column_sums[:model_width], column_sums[2 * model_width :]])
    grad_w_qkv = left_product(normed_first, grad_projected)
    grad_normed_first = right_product(grad_projected, w_qkv)
    first_pull = jax.vjp(layer_norm, inputs, ln1_gain, ln1_bias)[1]
    grad_in_norm, grad_ln1_gain, grad_ln1_bias = first_pull(grad_normed_first)
    grad_input = grad_middle + grad_in_norm
    summed = (
        lax.psum_scatter(grad_ln1_gain, ("seq", "hd"), scatter_dimension=0, tiled=True),
        lax.psum_scatter(grad_ln1_bias, ("seq", "hd"), scatter_dimension=0, tiled=True),
        lax.psum_scatter(grad_w_qkv, ("seq", "hd"), scatter_dimension=0, tiled=True),
        lax.psum_scatter(grad_qv_bias, ("seq", "hd"), scatter_dimension=0, tiled=True),
        lax.psum_scatter(grad_w_out, ("seq", "hd"), scatter_dimension=0, tiled=True),
        lax.psum_scatter(grad_b_out, ("seq", "hd"), scatter_dimension=0, tiled=True),
        lax.psum_scatter(grad_ln2_gain, ("seq", "hd"), scatter_dimension=0, tiled=True),
        lax.psum_scatter(grad_ln2_bias, ("seq", "hd"), scatter_dimension=0, tiled=True),
        lax.psum_scatter(grad_w_fc1, ("seq", "hd"), scatter_dimension=0, tiled=True),
        lax.psum_scatter(grad_b_fc1, ("seq", "hd"), scatter_dimension=0, tiled=True),
        lax.psum_scatter(grad_w_fc2, ("seq", "hd"), scatter_dimension=0, tiled=True),
        lax.psum_scatter(grad_b_fc2, ("seq", "hd"), scatter_dimension=0, tiled=True),
    )
    return (
        mixed_out,
        grad_input,
        summed[0],
        summed[1],
        summed[2],
        summed[3],
        summed[4],
        summed[5],
        summed[6],
        summed[7],
        summed[8],
        summed[9],
        summed[10],
        summed[11],
    )


def solution(mesh):
    placed = (
        P(("seq", "hd"), None),
        P(("seq", "hd")),
        P("seq", None, None),
        P(),
        P(),
        P(),
        P(),
        P(),
        P(),
        P(),
        P(),
        P(),
        P(),
        P(),
        P(),
        P(("seq", "hd"), None),
    )
    return jax.shard_map(
        per_device,
        mesh=mesh,
        in_specs=placed,
        out_specs=(
            P(("seq", "hd"), None),
            P(("seq", "hd"), None),
            P(("seq", "hd")),
            P(("seq", "hd")),
            P(("seq", "hd"), None),
            P(("seq", "hd")),
            P(("seq", "hd"), None),
            P(("seq", "hd")),
            P(("seq", "hd")),
            P(("seq", "hd")),
            P(("seq", "hd"), None),
            P(("seq", "hd")),
            P(("seq", "hd"), None),
            P(("seq", "hd")),
        ),
        check_vma=False,
    )
```

profile of v0, /device:TPU:0, one launch (start us, length us, event | category | flops | bytes accessed | tf_op | source)
XLA Modules:
  0.0 1052.6 jit_solution(14303516046795119364)
XLA Ops:
  25.6 7.7 reshape.282
  37.6 5.8 all-to-all-start.1
  44.7 39.6 %all-to-all-done.1 = bf16[768,3,2,384]{3,0,1,2:T(8,128)(2,1)} async-done(((bf16[768,3,2,384]{3,0,1,2:T(8,128)(2,1)}), bf16[768,3,2,384]{3,0,1,2:T(8,128)(2,1)}, u32[]{:S(2)}, u32[]{:S(2)}) %all-to-all-start.1) | async-done | bytes 3538976 | tf_op jit(solution)/shard_map/all_to_all | solution.py:158
  84.3 12.0 %copy.97 = bf16[2,768,3,1,384]{1,0,4,2,3:T(2,128)(2,1)} copy(bf16[2,768,3,1,384]{4,1,2,0,3:T(8,128)(2,1)} %bitcast.7) | data formatting | bytes 7077888 | tf_op jit(solution)/shard_map/all_to_all | solution.py:158
  96.3 8.8 reshape.283
  110.1 65.6 %while.27 = (s32[]{:T(128)}, bf16[3,512,6,64]{1,3,2,0:T(8,128)(2,1)}, f32[3,6,512]{2,1,0:T(8,128)}, s32[3]{0:T(128)S(1)}, bf16[1536]{0:T(1024)(128)(2,1)}, /*ind...) while((s32[]{:T(128)}, ...), condition=%wide.region_5.6_spmd, body=%wide.region_2.5_spmd.sunk | while | flops 1265366016 | bytes 66569444 | solution.py:71
  113.4 5.6 fusion.124
  119.0 4.9 fusion.125
  124.4 7.6 fusion.126
  135.2 5.6 fusion.124
  146.3 7.6 fusion.126
  157.1 5.6 fusion.124
  168.2 7.6 fusion.126
  180.4 8.6 reshape.288
  189.0 11.1 %reduce.9 = bf16[1536,384]{1,0:T(8,128)(2,1)} reduce(bf16[1536,1,384]{2,1,0:T(2,128)(2,1)} %reshape.288, bf16[]{:T(256)} %broadcast.224), dimensions={1}, to_apply=%reshape.288.reduce_sub_computation | reduce | bytes 2359298 | tf_op jit(solution)/shard_map/convert_element_type | solution.py:175
  209.9 12.0 %all-to-all-done.2 = bf16[2,2,147456]{2,1,0:T(2,128)(2,1)} async-done(((bf16[2,2,147456]{2,1,0:T(2,128)(2,1)}), bf16[2,2,147456]{2,1,0:T(2,128)(2,1)}, u32[]{:S(2)}, u32[]{:S(2)}) %all-to-all-start.2) | async-done | bytes 1179680 | tf_op jit(solution)/shard_map/all_to_all | solution.py:176
  235.2 27.6 %multiply_convert_fusion.1 = (bf16[768,3072]{1,0:T(8,128)(2,1)}, f32[768,3072]{1,0:T(8,128)}, f32[768,3072]{1,0:T(8,128)}) fusion(f32[3072]{0:T(1024)S(1)} %copy-done.45, bf16[768,3072]{1,0:T(8,128)(2,1)S(1)} %bitcast.139, f32[768,768]{0,1:T(8,128)S(1)} %get-tuple-element.316, f32[768]{0:T(1024)S(1)} %copy-done.49, f32[768]{0:T(1024)S(1)} %copy-done.38, ...), kind=kOutput, calls=%fused_computation.47 | convolution fusion | flops 3782541312 | bytes 30695424 | tf_op jit(solution)/shard_map/dot_general | solution.py:182
  262.9 13.3 %convert_reduce_fusion = (f32[3072]{0:T(1024)}, bf16[768,3072]{1,0:T(8,128)(2,1)}) fusion(f32[768,3072]{1,0:T(8,128)} %get-tuple-element.301, bf16[3072,768]{1,0:T(8,128)(2,1)S(1)} %bitcast.141, bf16[768,768]{0,1:T(8,128)(2,1)S(1)} %copy-done.14, f32[768]{0:T(1024)S(1)} %get-tuple-element.244, f32[768,3072]{1,0:T(8,128)} %get-tuple-element.317, ...), kind=kOutput, calls=%fused_computation.45 | convolution fusion | flops 3665753088 | bytes 29518848 | tf_op jit(solution)/shard_map/dot_general | solution.py:32
  276.2 8.3 fusion.77
  305.0 9.5 all-to-all-done.3
  323.5 226.6 %while.28 = (s32[]{:T(128)}, f32[1536,6,64]{0,2,1:T(8,128)}, f32[1536,6,64]{0,2,1:T(8,128)}, bf16[3,512,6,64]{1,3,2,0:T(8,128)(2,1)}, s32[3]{0:T(128)}, /*index=...) while((s32[]{:T(128)}, f32[1536,6,64]{0,2,1:T(8,128)}, ...), condition=%wide.region_12.13_spmd.clone, body=%wide.region_10.12_spmd.clone.sunk | while | flops 3094606848 | bytes 218333664 | solution.py:111
  325.6 10.6 %fusion.136 = f32[6,512,1536]{2,1,0:T(8,128)} fusion(bf16[1536,6,64]{0,2,1:T(8,128)(2,1)} %get-tuple-element.546, bf16[1536,6,64]{0,2,1:T(8,128)(2,1)} %get-tuple-element.543, s32[]{:T(128)S(6)} %select_n.64), kind=kOutput, calls=%fused_computation.34.clone.1 | convolution fusion | flops 603979776 | bytes 20447236 | tf_op jit(solution)/shard_map/while/body/eval_jaxpr/qhd,khd->hqk/dot_general | solution.py:45
  341.7 16.7 %multiply_reduce_fusion.5 = (f32[6,512]{1,0:T(8,128)S(1)}, f32[6,512,1536]{2,1,0:T(8,128)}) fusion(f32[6,512,1536]{2,1,0:T(8,128)} %fusion.136, f32[6,512]{1,0:T(8,128)S(1)} %dynamic-slice_bitcast_fusion.2, pred[512,1536]{1,0:T(8,128)(4,1)} %broadcast_compare_fusion.5, bf16[1536,6,64]{0,2,1:T(8,128)(2,1)} %get-tuple-element.549, ...), kind=kOutput, calls=%fused_computation.16.clone.1 | convolution fusion | flops 627569664 | bytes 40132612 | tf_op jit(solution)/shard_map/while/body/eval_jaxpr/qhd,khd->hqk/dot_general | solution.py:91
  358.4 17.2 %multiply_convert_fusion.5 = bf16[6,512,1536]{2,1,0:T(8,128)(2,1)} fusion(f32[6,512,1536]{2,1,0:T(8,128)} %get-tuple-element.458, f32[6,512,1536]{2,1,0:T(8,128)} %fusion.136, f32[6,512]{1,0:T(8,128)S(1)} %get-tuple-element.459, f32[6,512]{1,0:T(8,128)S(1)} %dynamic-slice_bitcast_fusion.2, pred[512,1536]{1,0:T(8,128)(4,1)S(1)} %copy-done.4), kind=kLoop, calls=%fused_computation.15.clone.1 | loop fusion | flops 28311552 | bytes 47996928 | tf_op jit(solution)/shard_map/while/body/eval_jaxpr/convert_element_type | solution.py:95
  375.6 7.3 fusion.137
  387.7 10.8 %fusion.138 = f32[1536,6,64]{0,2,1:T(8,128)} fusion(f32[6,512,1536]{2,1,0:T(8,128)} %fusion.136, f32[6,512]{1,0:T(8,128)S(1)} %dynamic-slice_bitcast_fusion.2, pred[512,1536]{1,0:T(8,128)(4,1)S(1)} %copy-done.5, f32[1536,6,64]{0,2,1:T(8,128)} %get-tuple-element.522, pred[]{:T(512)S(6)} %compare.3, bf16[1536,6,64]{0,2,1:T(8,128)(2,1)} %get-tuple-element.548, ...), kind=kOutput, calls=%fused_computation.25.clone.1 | convolution fusion | flops 624033792 | bytes 24784900 | tf_op jit(solution)/shard_map/while/body/eval_jaxpr/hqk,qhd->khd/dot_general | solution.py:105
  400.3 10.5 %fusion.136 = f32[6,512,1536]{2,1,0:T(8,128)} fusion(bf16[1536,6,64]{0,2,1:T(8,128)(2,1)} %get-tuple-element.546, bf16[1536,6,64]{0,2,1:T(8,128)(2,1)} %get-tuple-element.543, s32[]{:T(128)S(6)} %select_n.64), kind=kOutput, calls=%fused_computation.34.clone.1 | convolution fusion | flops 603979776 | bytes 20447236 | tf_op jit(solution)/shard_map/while/body/eval_jaxpr/qhd,khd->hqk/dot_general | solution.py:45
  416.4 16.7 %multiply_reduce_fusion.5 = (f32[6,512]{1,0:T(8,128)S(1)}, f32[6,512,1536]{2,1,0:T(8,128)}) fusion(f32[6,512,1536]{2,1,0:T(8,128)} %fusion.136, f32[6,512]{1,0:T(8,128)S(1)} %dynamic-slice_bitcast_fusion.2, pred[512,1536]{1,0:T(8,128)(4,1)} %broadcast_compare_fusion.5, bf16[1536,6,64]{0,2,1:T(8,128)(2,1)} %get-tuple-element.549, ...), kind=kOutput, calls=%fused_computation.16.clone.1 | convolution fusion | flops 627569664 | bytes 40132612 | tf_op jit(solution)/shard_map/while/body/eval_jaxpr/qhd,khd->hqk/dot_general | solution.py:91
  433.1 17.1 %multiply_convert_fusion.5 = bf16[6,512,1536]{2,1,0:T(8,128)(2,1)} fusion(f32[6,512,1536]{2,1,0:T(8,128)} %get-tuple-element.458, f32[6,512,1536]{2,1,0:T(8,128)} %fusion.136, f32[6,512]{1,0:T(8,128)S(1)} %get-tuple-element.459, f32[6,512]{1,0:T(8,128)S(1)} %dynamic-slice_bitcast_fusion.2, pred[512,1536]{1,0:T(8,128)(4,1)S(1)} %copy-done.4), kind=kLoop, calls=%fused_computation.15.clone.1 | loop fusion | flops 28311552 | bytes 47996928 | tf_op jit(solution)/shard_map/while/body/eval_jaxpr/convert_element_type | solution.py:95
  450.2 7.8 fusion.137
  462.8 11.4 %fusion.138 = f32[1536,6,64]{0,2,1:T(8,128)} fusion(f32[6,512,1536]{2,1,0:T(8,128)} %fusion.136, f32[6,512]{1,0:T(8,128)S(1)} %dynamic-slice_bitcast_fusion.2, pred[512,1536]{1,0:T(8,128)(4,1)S(1)} %copy-done.5, f32[1536,6,64]{0,2,1:T(8,128)} %get-tuple-element.522, pred[]{:T(512)S(6)} %compare.3, bf16[1536,6,64]{0,2,1:T(8,128)(2,1)} %get-tuple-element.548, ...), kind=kOutput, calls=%fused_computation.25.clone.1 | convolution fusion | flops 624033792 | bytes 24784900 | tf_op jit(solution)/shard_map/while/body/eval_jaxpr/hqk,qhd->khd/dot_general | solution.py:105
  476.1 10.5 %fusion.136 = f32[6,512,1536]{2,1,0:T(8,128)} fusion(bf16[1536,6,64]{0,2,1:T(8,128)(2,1)} %get-tuple-element.546, bf16[1536,6,64]{0,2,1:T(8,128)(2,1)} %get-tuple-element.543, s32[]{:T(128)S(6)} %select_n.64), kind=kOutput, calls=%fused_computation.34.clone.1 | convolution fusion | flops 603979776 | bytes 20447236 | tf_op jit(solution)/shard_map/while/body/eval_jaxpr/qhd,khd->hqk/dot_general | solution.py:45
  492.1 16.7 %multiply_reduce_fusion.5 = (f32[6,512]{1,0:T(8,128)S(1)}, f32[6,512,1536]{2,1,0:T(8,128)}) fusion(f32[6,512,1536]{2,1,0:T(8,128)} %fusion.136, f32[6,512]{1,0:T(8,128)S(1)} %dynamic-slice_bitcast_fusion.2, pred[512,1536]{1,0:T(8,128)(4,1)} %broadcast_compare_fusion.5, bf16[1536,6,64]{0,2,1:T(8,128)(2,1)} %get-tuple-element.549, ...), kind=kOutput, calls=%fused_computation.16.clone.1 | convolution fusion | flops 627569664 | bytes 40132612 | tf_op jit(solution)/shard_map/while/body/eval_jaxpr/qhd,khd->hqk/dot_general | solution.py:91
  508.8 17.1 %multiply_convert_fusion.5 = bf16[6,512,1536]{2,1,0:T(8,128)(2,1)} fusion(f32[6,512,1536]{2,1,0:T(8,128)} %get-tuple-element.458, f32[6,512,1536]{2,1,0:T(8,128)} %fusion.136, f32[6,512]{1,0:T(8,128)S(1)} %get-tuple-element.459, f32[6,512]{1,0:T(8,128)S(1)} %dynamic-slice_bitcast_fusion.2, pred[512,1536]{1,0:T(8,128)(4,1)S(1)} %copy-done.4), kind=kLoop, calls=%fused_computation.15.clone.1 | loop fusion | flops 28311552 | bytes 47996928 | tf_op jit(solution)/shard_map/while/body/eval_jaxpr/convert_element_type | solution.py:95
  526.0 7.8 fusion.137
  538.5 11.4 %fusion.138 = f32[1536,6,64]{0,2,1:T(8,128)} fusion(f32[6,512,1536]{2,1,0:T(8,128)} %fusion.136, f32[6,512]{1,0:T(8,128)S(1)} %dynamic-slice_bitcast_fusion.2, pred[512,1536]{1,0:T(8,128)(4,1)S(1)} %copy-done.5, f32[1536,6,64]{0,2,1:T(8,128)} %get-tuple-element.522, pred[]{:T(512)S(6)} %compare.3, bf16[1536,6,64]{0,2,1:T(8,128)(2,1)} %get-tuple-element.548, ...), kind=kOutput, calls=%fused_computation.25.clone.1 | convolution fusion | flops 624033792 | bytes 24784900 | tf_op jit(solution)/shard_map/while/body/eval_jaxpr/hqk,qhd->khd/dot_general | solution.py:105
  563.1 8.2 copy.106
  571.3 55.3 %all_to_all.78 = bf16[1536,3,1,384]{3,1,2,0:T(4,128)(2,1)S(1)} all-to-all(bf16[1536,3,1,384]{3,1,2,0:T(4,128)(2,1)} %copy.106), channel_id=1, replica_groups=mesh['seq'=16,'hd'=2] {'hd'}, dimensions={0} | all-to-all | bytes 7077888 | tf_op jit(solution)/shard_map/all_to_all | solution.py:214
  628.8 6.1 copy.108
  634.9 8.4 fusion.66
  644.0 10.7 %fusion.69 = f32[768,3072]{1,0:T(8,128)} fusion(bf16[768,3072]{1,0:T(8,128)(2,1)} %get-tuple-element.323, f32[768,768]{0,1:T(8,128)} %copy-done.9, f32[768]{0:T(1024)} %param.30, f32[768]{0:T(1024)} %param.29, f32[768]{0:T(1024)} %copy-done.34, f32[768]{0:T(1024)S(1)} %copy-done.25), kind=kOutput, calls=%fused_computation.120 | convolution fusion | flops 3626827776 | bytes 16527360 | tf_op jit(solution)/shard_map/dot_general | solution.py:26
  655.3 10.5 fusion.54
  665.8 9.8 add_convert_fusion.2
  683.3 7.0 fusion.76
  703.1 41.3 %all-reduce.8 = (f32[768]{0:T(1024)}, f32[768]{0:T(1024)}, f32[1536]{0:T(1024)}, f32[768]{0:T(1024)}, f32[768]{0:T(1024)}, /*index=5*/f32[768]{0:T(1024)}, f32[3072]{0:T(1024)S(1)}, f32[768]{0:T(1024)S(1)}) all-reduce(f32[768]{0:T(1024)} %get-tuple-element.242, ...), channel_id=2, replica_groups=mesh['seq'=16,'hd'=2] {'seq','hd'}, use_global_device_ids=true, to_apply=%region_16.17.clone | all-reduce | flops 9216 | bytes 73728
  756.2 6.4 reduce-scatter.5.cloned.1.call-done
  762.6 141.2 %reduce-scatter.9.cloned.1.call-done = f32[24,3072]{1,0:T(8,128)} async-done(((f32[768,3072]{1,0:T(8,128)}), f32[24,3072]{1,0:T(8,128)}) %reduce-scatter.9.cloned.1.call-update) | async-done | bytes 294928 | tf_op jit(solution)/shard_map/reduce_scatter | solution.py:233
  903.8 142.0 %reduce-scatter.11.cloned.1.call-done = f32[96,768]{1,0:T(8,128)} async-done(((f32[3072,768]{1,0:T(8,128)}), f32[96,768]{1,0:T(8,128)}) %reduce-scatter.11.cloned.1.call-update) | async-done | bytes 294928 | tf_op jit(solution)/shard_map/reduce_scatter | solution.py:235
  (264 shorter events, 182.7 us)
Async XLA Ops:
  7.2 13.7 %copy-start = (bf16[768,2304]{1,0:T(8,128)(2,1)S(1)}, bf16[768,2304]{1,0:T(8,128)(2,1)}, u32[]{:S(2)}) copy-start(bf16[768,2304]{1,0:T(8,128)(2,1)} %param.25) | copy-start | bytes 10616836
  9.8 27.8 %all-to-all-start = ((bf16[2,2,384]{2,1,0:T(2,128)(2,1)}), bf16[2,2,384]{2,1,0:T(2,128)(2,1)S(1)}, u32[]{:S(2)}, u32[]{:S(2)}) async-start(bf16[2,2,384]{2,1,0:T(2,128)(2,1)} %reshape.293), calls=%async_computation | async-start | bytes 6144 | tf_op jit(solution)/shard_map/all_to_all | solution.py:165
  14.0 6.2 copy-start.42
  14.0 6.8 copy-start.30
  16.4 4.4 copy-start.6
  16.4 4.4 copy-start.47
  37.6 46.7 %all-to-all-start.1 = ((bf16[768,3,2,384]{3,0,1,2:T(8,128)(2,1)}), bf16[768,3,2,384]{3,0,1,2:T(8,128)(2,1)}, u32[]{:S(2)}, u32[]{:S(2)}) async-start(bf16[768,3,2,384]{3,0,1,2:T(8,128)(2,1)} %copy.96), calls=%async_computation.1 | async-start | bytes 7077888 | tf_op jit(solution)/shard_map/all_to_all | solution.py:158
  113.4 5.6 copy-start.3
  135.2 5.6 copy-start.3
  157.1 5.6 copy-start.3
  202.4 7.2 copy-start.43
  202.4 7.2 copy-start.50
  202.4 19.5 %all-to-all-start.2 = ((bf16[2,2,147456]{2,1,0:T(2,128)(2,1)}), bf16[2,2,147456]{2,1,0:T(2,128)(2,1)}, u32[]{:S(2)}, u32[]{:S(2)}) async-start(bf16[2,2,147456]{2,1,0:T(2,128)(2,1)} %reshape.295), calls=%async_computation.2 | async-start | bytes 2359296 | tf_op jit(solution)/shard_map/all_to_all | solution.py:176
  209.9 20.4 %copy-start.40 = (f32[768]{0:T(1024)}, f32[768]{0:T(1024)S(1)}, u32[]{:S(2)}) copy-start(f32[768]{0:T(1024)S(1)} %get-tuple-element.245) | copy-start | bytes 9220
  209.9 52.9 %copy-start.35 = (f32[768]{0:T(1024)}, f32[768]{0:T(1024)S(1)}, u32[]{:S(2)}) copy-start(f32[768]{0:T(1024)S(1)} %get-tuple-element.244) | copy-start | bytes 9220
  225.0 5.3 copy-start.46
  230.3 32.6 %slice-start.2 = ((s8[4718592]{0:T(1024)(128)(4,1)}), s8[4194304]{0:T(1024)(128)(4,1)S(1)}, s32[]{:S(2)}) async-start(s8[4718592]{0:T(1024)(128)(4,1)} %bitcast.140), calls=%async_computation.15 | async-start | bytes 8388608
  233.8 29.1 %copy-start.9 = (f32[768,768]{0,1:T(8,128)}, f32[768,768]{0,1:T(8,128)S(1)}, u32[]{:S(2)}) copy-start(f32[768,768]{0,1:T(8,128)S(1)} %get-tuple-element.316) | copy-start | bytes 7077892
  233.8 57.5 %copy-start.24 = (f32[768]{0:T(1024)}, f32[768]{0:T(1024)S(1)}, u32[]{:S(2)}) copy-start(f32[768]{0:T(1024)S(1)} %broadcast_multiply_fusion) | copy-start | bytes 9220
  235.2 56.2 %copy-start.34 = (f32[768]{0:T(1024)}, f32[768]{0:T(1024)S(1)}, u32[]{:S(2)}) copy-start(f32[768]{0:T(1024)S(1)} %fusion.63) | copy-start | bytes 9220
  235.2 27.7 %copy-start.14 = (bf16[768,768]{0,1:T(8,128)(2,1)S(1)}, bf16[768,768]{0,1:T(8,128)(2,1)}, u32[]{:S(2)}) copy-start(bf16[768,768]{0,1:T(8,128)(2,1)} %copy.102) | copy-start | bytes 3538948
  235.2 27.7 %slice-start.3 = ((s8[4718592]{0:T(1024)(128)(4,1)}), s8[524288]{0:T(1024)(128)(4,1)S(1)}, s32[]{:S(2)}) async-start(s8[4718592]{0:T(1024)(128)(4,1)} %bitcast.140), calls=%async_computation.16 | async-start | bytes 1048576
  296.2 18.3 %all-to-all-start.3 = ((bf16[768,2,384]{0,2,1:T(8,128)(2,1)}), bf16[768,2,384]{0,2,1:T(8,128)(2,1)}, u32[]{:S(2)}, u32[]{:S(2)}) async-start(bf16[768,2,384]{0,2,1:T(8,128)(2,1)} %bitcast.134), calls=%async_computation.3 | async-start | bytes 2359296 | tf_op jit(solution)/shard_map/all_to_all | solution.py:203
  300.7 455.5 %reduce-scatter.7.cloned.1.call-start = ((), (), s32[]{:S(2)}) async-start(), calls=%async_computation.10 | async-start | bytes 2433024 | tf_op jit(solution)/shard_map/reduce_scatter | solution.py:229
  305.0 457.6 %reduce-scatter.5.cloned.1.call-start = ((), (), s32[]{:S(2)}) async-start(), calls=%async_computation.9 | async-start | bytes 7299072 | tf_op jit(solution)/shard_map/reduce_scatter | solution.py:227
  341.7 16.7 %copy-start.4 = (pred[512,1536]{1,0:T(8,128)(4,1)S(1)}, pred[512,1536]{1,0:T(8,128)(4,1)}, u32[]{:S(2)}) copy-start(pred[512,1536]{1,0:T(8,128)(4,1)} %broadcast_compare_fusion.5) | copy-start | bytes 2359300 | tf_op jit(solution)/shard_map/while
  375.6 7.3 copy-start.1
  375.6 7.3 copy-start.2
  375.6 8.1 copy-start.18
  383.7 4.0 copy-start.5
  416.4 16.7 %copy-start.4 = (pred[512,1536]{1,0:T(8,128)(4,1)S(1)}, pred[512,1536]{1,0:T(8,128)(4,1)}, u32[]{:S(2)}) copy-start(pred[512,1536]{1,0:T(8,128)(4,1)} %broadcast_compare_fusion.5) | copy-start | bytes 2359300 | tf_op jit(solution)/shard_map/while
  450.2 7.8 copy-start.1
  450.2 7.8 copy-start.2
  450.2 8.6 copy-start.18
  492.1 16.7 %copy-start.4 = (pred[512,1536]{1,0:T(8,128)(4,1)S(1)}, pred[512,1536]{1,0:T(8,128)(4,1)}, u32[]{:S(2)}) copy-start(pred[512,1536]{1,0:T(8,128)(4,1)} %broadcast_compare_fusion.5) | copy-start | bytes 2359300 | tf_op jit(solution)/shard_map/while
  526.0 7.8 copy-start.1
  526.0 7.8 copy-start.2
  526.0 8.6 copy-start.18
  534.6 4.0 copy-start.5
  628.8 6.1 copy-start.23
  628.8 6.1 copy-start.27
  628.8 6.1 copy-start.31
  628.8 6.1 copy-start.48
  643.3 260.5 %reduce-scatter.9.cloned.1.call-start = ((), (), s32[]{:S(2)}) async-start(), calls=%async_computation.11 | async-start | bytes 9732096 | tf_op jit(solution)/shard_map/reduce_scatter | solution.py:233
  654.7 391.2 %reduce-scatter.11.cloned.1.call-start = ((), (), s32[]{:S(2)}) async-start(), calls=%async_computation.12 | async-start | bytes 9732096 | tf_op jit(solution)/shard_map/reduce_scatter | solution.py:235
  693.3 4.5 copy-start.29
  693.3 4.6 copy-start.7
  693.3 4.6 copy-start.8
  (29 other events, 55.7 us)
Sparse Core Ops, SparseCore 0:
  307.4 100.7 reduce-scatter.6
  643.5 119.0 reduce-scatter.4
  769.1 134.7 reduce-scatter.8
  911.2 134.6 reduce-scatter.10
where the time goes:
time: 1060 us; the launch traced here: 1050 us
  waiting for transfers between devices  351 us (33%)
  matrix products  297 us (28%)
  local copies, waits for them, and re-layouts  148 us (14%)
  other arithmetic  116 us (11%)
  blocking collectives  96.6 us (9%)
  starting transfers between devices  19.8 us (2%)
  between operations  14.5 us (1%)
    reduce_scatter x1, waiting for transfers between devices, per_device(): lax.psum_scatter(grad_w_fc2, ('seq', 'hd'), scatter_dimension=0, tiled=True)  142 us
    reduce_scatter x1, waiting for transfers between devices, per_device(): lax.psum_scatter(grad_w_fc1, ('seq', 'hd'), scatter_dimension=0, tiled=True)  141 us
    all_to_all x1, blocking collectives, per_device(): lax.all_to_all(stacked.reshape(group_rows, 3, 1, head_width), 'hd', split...  55.3 us
    convert_element_type x3, other arithmetic, one_block(): grad_low = grad_scores.astype(jnp.bfloat16)  51.5 us
    dot_general x3, matrix products, one_block(): jnp.einsum('qhd,khd->hqk', grad_rows, values_all, preferred_element_type=...  50.1 us
    dot_general x6, matrix products, block_scores(): jnp.einsum('qhd,khd->hqk', query_rows, keys_all, preferred_element_type=j...  48.4 us
    unnamed x1, blocking collectives  41.3 us
    all_to_all x1, waiting for transfers between devices, per_device(): lax.all_to_all(projected.reshape(tok_rows, 3, pair_count, head_width), 'h...  39.6 us
  transfers between devices with their start and end apart: 8, of which 6 were waited for; matrix products, arithmetic and copies ran while one was open for 34% of the time, Pallas kernels for 0%

commit v1 on v0

v1 whole, which is shorter than its diff:
```python
import functools
import jax, jax.numpy as jnp
from jax import lax
from jax.experimental import pallas as pl
from jax.experimental.pallas import tpu as pltpu
from jax.sharding import PartitionSpec as P

HEADS, HEAD = 12, 64
T = 128
VM = pl.BlockSpec(memory_space=pltpu.VMEM)
SM = pl.BlockSpec(memory_space=pltpu.SMEM)
F32, BF16 = jnp.float32, jnp.bfloat16
NT = (((1,), (1,)), ((), ()))
TN = (((0,), (0,)), ((), ()))


def mm(a, b):
    return jnp.dot(a, b, preferred_element_type=F32)


def mm_nt(a, b):
    return lax.dot_general(a, b, NT, preferred_element_type=F32)


def mm_tn(a, b):
    return lax.dot_general(a, b, TN, preferred_element_type=F32)


def by_head(pair):
    lane = lax.broadcasted_iota(jnp.int32, pair.shape, 1)
    zero = jnp.zeros_like(pair)
    return jnp.concatenate(
        [jnp.where(lane < HEAD, pair, zero), jnp.where(lane < HEAD, zero, pair)], 0
    )


def attn_forward_kernel(width, tiles, low_ref, high_ref, off_ref, qkv, id_col, id_row, out, lse, sc, peak, total, acc):
    pairs = width // 128
    own = out.shape[0] // T
    off = off_ref[0]

    @pl.loop(0, own)
    def _(i):
        tile = off + i
        q0 = pl.multiple_of(tile * T, T)
        low, high = low_ref[tile], high_ref[tile]
        ids = id_col[pl.ds(q0, T), :]
        for p in range(pairs):
            peak[p] = jnp.full((T, 2 * T), -jnp.inf, F32)
            total[p] = jnp.zeros((T, 2 * T), F32)
            acc[p] = jnp.zeros((T, 128), F32)

        @pl.loop(low, high)
        def _(j):
            k0 = pl.multiple_of(j * T, T)
            same = ids == id_row[j]
            for p in range(pairs):
                q = qkv[pl.ds(q0, T), p * 128 : p * 128 + 128] * BF16(HEAD**-0.5)
                k = by_head(qkv[pl.ds(k0, T), width + p * 128 : width + p * 128 + 128])
                s = mm_nt(q, k)
                s = jnp.concatenate([jnp.where(same, s[:, :T], -1e30), jnp.where(same, s[:, T:], -1e30)], 1)
                sc[p, j - low] = s
                peak[p] = jnp.maximum(peak[p], s)

        for p in range(pairs):
            m = peak[p]
            peak[p] = jnp.concatenate(
                [
                    jnp.broadcast_to(jnp.max(m[:, :T], -1, keepdims=True), (T, T)),
                    jnp.broadcast_to(jnp.max(m[:, T:], -1, keepdims=True), (T, T)),
                ],
                1,
            )

        @pl.loop(low, high)
        def _(j):
            k0 = pl.multiple_of(j * T, T)
            for p in range(pairs):
                v = by_head(qkv[pl.ds(k0, T), 2 * width + p * 128 : 2 * width + p * 128 + 128])
                e = jnp.exp(sc[p, j - low] - peak[p])
                total[p] += e
                acc[p] += mm(e.astype(BF16), v)

        lane = lax.broadcasted_iota(jnp.int32, (T, 128), 1)
        gathered = jnp.zeros((T, 128), F32)
        for p in range(pairs):
            t = total[p]
            t0 = jnp.sum(t[:, :T], -1, keepdims=True)
            t1 = jnp.sum(t[:, T:], -1, keepdims=True)
            inv = jnp.where(lane < HEAD, 1.0 / t0, 1.0 / t1)
            out[pl.ds(pl.multiple_of(i * T, T), T), p * 128 : p * 128 + 128] = (acc[p] * inv).astype(BF16)
            l0 = peak[p][:, 0:1] + jnp.log(t0)
            l1 = peak[p][:, T : T + 1] + jnp.log(t1)
            gathered = jnp.where(lane == 2 * p, l0, jnp.where(lane == 2 * p + 1, l1, gathered))
        lse[i] = gathered.T[: lse.shape[1], :]


def attn_forward(low, high, off, qkv, id_col, id_row, own_rows):
    all_rows, columns = qkv.shape
    width = columns // 3
    tiles = all_rows // T
    pairs = width // 128
    return pl.pallas_call(
        functools.partial(attn_forward_kernel, width, tiles),
        out_shape=(
            jax.ShapeDtypeStruct((own_rows, width), BF16),
            jax.ShapeDtypeStruct((own_rows // T, 16, T), F32),
        ),
        in_specs=[SM, SM, SM, VM, VM, VM],
        out_specs=(VM, VM),
        scratch_shapes=[
            pltpu.VMEM((pairs, tiles, T, 2 * T), F32),
            pltpu.VMEM((pairs, T, 2 * T), F32),
            pltpu.VMEM((pairs, T, 2 * T), F32),
            pltpu.VMEM((pairs, T, 128), F32),
        ],
        compiler_params=pltpu.CompilerParams(vmem_limit_bytes=56 * 2**20),
        name="attention_forward",
    )(low, high, off, qkv, id_col, id_row)


def attn_backward_kernel(width, tiles, low_ref, high_ref, off_ref, qkv, do, id_col, id_row, lse, delta, out, dq, dk, dv):
    pairs = width // 128
    own = out.shape[0] // T
    off = off_ref[0]
    dq[...] = jnp.zeros_like(dq)

    @pl.loop(0, tiles)
    def _(j):
        k0 = pl.multiple_of(j * T, T)
        mine = jnp.logical_and(j >= off, j < off + own)
        low = jnp.where(mine, low_ref[j], jnp.maximum(low_ref[j], off))
        high = jnp.where(mine, high_ref[j], jnp.minimum(high_ref[j], off + own))
        ids = id_col[pl.ds(k0, T), :]
        for p in range(pairs):
            dk[p] = jnp.zeros((T, 128), F32)
            dv[p] = jnp.zeros((T, 128), F32)

        @pl.loop(low, high)
        def _(i):
            q0 = pl.multiple_of(i * T, T)
            same = ids == id_row[i]
            for p in range(pairs):
                cols = p * 128
                k = qkv[pl.ds(k0, T), width + cols : width + cols + 128]
                v = qkv[pl.ds(k0, T), 2 * width + cols : 2 * width + cols + 128]
                q = by_head(qkv[pl.ds(q0, T), cols : cols + 128] * BF16(HEAD**-0.5))
                g = by_head(do[pl.ds(q0, T), cols : cols + 128])
                s = mm_nt(k, q)
                dp = mm_nt(v, g)
                es, ds = [], []
                for h in range(2):
                    sh = jnp.where(same, s[:, h * T : h * T + T], -1e30)
                    e = jnp.exp(sh - lse[i, 2 * p + h : 2 * p + h + 1, :])
                    es.append(e.astype(BF16))
                    ds.append((e * (dp[:, h * T : h * T + T] - delta[i, 2 * p + h : 2 * p + h + 1, :])).astype(BF16))
                dsc = jnp.concatenate(ds, 1)
                dv[p] += mm(jnp.concatenate(es, 1), g)
                dk[p] += mm(dsc, q)
                both = by_head(k)
                dq[i, :, cols : cols + 128] += mm_tn(jnp.concatenate(ds, 0), both)

        @pl.when(mine)
        def _():
            r0 = pl.multiple_of((j - off) * T, T)
            for p in range(pairs):
                cols = p * 128
                out[pl.ds(r0, T), width + cols : width + cols + 128] = dk[p].astype(BF16)
                out[pl.ds(r0, T), 2 * width + cols : 2 * width + cols + 128] = dv[p].astype(BF16)

    @pl.loop(0, own)
    def _(i):
        out[pl.ds(pl.multiple_of(i * T, T), T), 0:width] = (dq[off + i] * HEAD**-0.5).astype(BF16)


def attn_backward(low, high, off, qkv, do, id_col, id_row, lse, delta, own_rows):
    all_rows, columns = qkv.shape
    width = columns // 3
    tiles = all_rows // T
    pairs = width // 128
    return pl.pallas_call(
        functools.partial(attn_backward_kernel, width, tiles),
        out_shape=jax.ShapeDtypeStruct((own_rows, columns), BF16),
        in_specs=[SM, SM, SM] + [VM] * 6,
        out_specs=VM,
        scratch_shapes=[
            pltpu.VMEM((tiles, T, width), F32),
            pltpu.VMEM((pairs, T, 128), F32),
            pltpu.VMEM((pairs, T, 128), F32),
        ],
        compiler_params=pltpu.CompilerParams(vmem_limit_bytes=56 * 2**20),
        name="attention_backward",
    )(low, high, off, qkv, do, id_col, id_row, lse, delta)


ln_epsilon = 1e-06
drop_scale = 1.0 / 0.9


MESH = pl.DeviceIdType.MESH


class Place:
    def __init__(self):
        self.seq = lax.axis_index("seq")
        self.x = lax.axis_index("hd")
        self.c = lax.rem(self.seq, 2)
        self.y = lax.rem(self.seq // 2, 2)
        self.z = self.seq // 4

    def partner(self, axis):
        if axis == "c":
            return (self.seq + 1 - 2 * self.c, self.x)
        if axis == "y":
            return (self.seq + 2 - 4 * self.y, self.x)
        return (self.seq, 1 - self.x)

    def level(self, step):
        return (lax.rem(self.z + step, 4) * 4 + lax.rem(self.seq, 4), self.x)

    def index(self, axis):
        return {"x": self.x, "y": self.y, "c": self.c}[axis]


def greet(place):
    barrier = pltpu.get_barrier_semaphore()
    others = [place.partner(a) for a in "cxy"] + [place.level(d) for d in (1, 2, 3)]
    for other in others:
        pl.semaphore_signal(barrier, inc=1, device_id=other, device_id_type=MESH)
    pl.semaphore_wait(barrier, len(others))


def send(source, target, send_sem, recv_sem, other):
    copy = pltpu.make_async_remote_copy(
        src_ref=source, dst_ref=target, send_sem=send_sem, recv_sem=recv_sem, device_id=other, device_id_type=MESH
    )
    copy.start()
    return copy


class Flow:
    def __init__(self, place, axes, g, r0, r1, r2, r3, sems, recvs):
        self.place, self.axes, self.g = place, axes, g
        self.r0, self.r1, self.r2, self.r3 = r0, r1, r2, r3
        self.sems, self.recvs = sems, recvs
        self.copies = []

    def start(self):
        p = self.place
        self.copies.append(send(self.g.at[1 - p.c], self.r0, self.sems.at[0], self.recvs.at[0], p.partner("c")))

    def first(self):
        p = self.place
        self.copies[0].wait_recv()
        me = p.index(self.axes[0])

        def add(half):
            @pl.loop(0, 8)
            def _(i):
                b, z = i // 4, lax.rem(i, 4)
                self.r0[half, b, z] = self.r0[half, b, z] + self.g[p.c, half, b, z]

        add(1 - me)
        self.copies.append(
            send(self.r0.at[1 - me], self.r1, self.sems.at[1], self.recvs.at[1], p.partner(self.axes[0]))
        )
        add(me)

    def second(self):
        p = self.place
        self.copies[1].wait_recv()
        me, before = p.index(self.axes[1]), p.index(self.axes[0])

        def add(half):
            @pl.loop(0, 4)
            def _(z):
                self.r1[half, z] = self.r1[half, z] + self.r0[before, half, z]

        add(1 - me)
        self.copies.append(
            send(self.r1.at[1 - me], self.r2, self.sems.at[2], self.recvs.at[2], p.partner(self.axes[1]))
        )
        add(me)

    def third(self):
        p = self.place
        self.copies[2].wait_recv()
        before = p.index(self.axes[1])

        @pl.loop(0, 4)
        def _(z):
            self.r2[z] = self.r2[z] + self.r1[before, z]

        for d in (1, 2, 3):
            target = lax.rem(p.z + d, 4)
            self.copies.append(
                send(self.r2.at[target], self.r3.at[d - 1], self.sems.at[2 + d], self.recvs.at[2 + d], p.level(d))
            )

    def last(self):
        p = self.place
        total = self.r2[p.z].astype(F32)
        for d in (1, 2, 3):
            self.copies[2 + d].wait_recv()
            total = total + self.r3[d - 1].astype(F32)
        return total

    def finish(self):
        for copy in self.copies:
            copy.wait_send()


def flow_scratch(rows, cols):
    return [
        pltpu.VMEM((2, 2, 4, rows, cols), BF16),
        pltpu.VMEM((2, 4, rows, cols), BF16),
        pltpu.VMEM((4, rows, cols), BF16),
        pltpu.VMEM((3, rows, cols), BF16),
        pltpu.SemaphoreType.DMA((6,)),
        pltpu.SemaphoreType.DMA((6,)),
    ]


class ChunkFlow(Flow):
    def __init__(self, place, axes, home, *refs):
        super().__init__(place, axes, *refs)
        self.home = home

    def third(self):
        p = self.place
        self.copies[2].wait_recv()
        self.r2[...] = self.r2[...] + self.r1[p.index(self.axes[1])]
        slot = lax.rem(p.z - self.home + 3, 4)
        self.hop = pltpu.make_async_remote_copy(
            src_ref=self.r2,
            dst_ref=self.r3.at[slot],
            send_sem=self.sems.at[3],
            recv_sem=self.recvs.at[3 + slot],
            device_id=(self.home * 4 + lax.rem(p.seq, 4), p.x),
            device_id_type=MESH,
        )

        @pl.when(p.z != self.home)
        def _():
            self.hop.start()

    def first(self):
        p = self.place
        self.copies[0].wait_recv()
        me = p.index(self.axes[0])

        def add(half):
            for b in range(2):
                self.r0[half, b] = self.r0[half, b] + self.g[p.c, half, b]

        add(1 - me)
        self.copies.append(
            send(self.r0.at[1 - me], self.r1, self.sems.at[1], self.recvs.at[1], p.partner(self.axes[0]))
        )
        add(me)

    def second(self):
        p = self.place
        self.copies[1].wait_recv()
        me, before = p.index(self.axes[1]), p.index(self.axes[0])
        self.r1[1 - me] = self.r1[1 - me] + self.r0[before, 1 - me]
        self.copies.append(
            send(self.r1.at[1 - me], self.r2, self.sems.at[2], self.recvs.at[2], p.partner(self.axes[1]))
        )
        self.r1[me] = self.r1[me] + self.r0[before, me]

    def last_into(self, out):
        p = self.place

        @pl.when(p.z == self.home)
        def _():
            total = self.r2[...].astype(F32)
            for slot in range(3):
                pltpu.make_async_remote_copy(
                    src_ref=self.r2,
                    dst_ref=self.r3.at[slot],
                    send_sem=self.sems.at[3],
                    recv_sem=self.recvs.at[3 + slot],
                    device_id=p.level(1),
                    device_id_type=MESH,
                ).wait_recv()
                total = total + self.r3[slot].astype(F32)
            out[...] = total

    def finish(self):
        super().finish()

        @pl.when(self.place.z != self.home)
        def _():
            self.hop.wait_send()


def chunk_scratch(rows, cols):
    return [
        pltpu.VMEM((2, 2, rows, cols), BF16),
        pltpu.VMEM((2, rows, cols), BF16),
        pltpu.VMEM((rows, cols), BF16),
        pltpu.VMEM((3, rows, cols), BF16),
        pltpu.SemaphoreType.DMA((6,)),
        pltpu.SemaphoreType.DMA((6,)),
    ]


def row_norm(x):
    mean = jnp.mean(x, -1, keepdims=True)
    center = x - mean
    rstd = lax.rsqrt(jnp.mean(center * center, -1, keepdims=True) + ln_epsilon)
    return center * rstd, rstd


def norm_back(hat, rstd, gain, grad):
    scaled = grad * gain
    return rstd * (scaled - jnp.mean(scaled, -1, keepdims=True) - hat * jnp.mean(scaled * hat, -1, keepdims=True))


def col_sum(x):
    return jnp.sum(x, 0, keepdims=True)


def put_blocks(product, z, axes, g):
    half = product.shape[1] // 2
    for y in range(2):
        for c in range(2):
            for x in range(2):
                r = ((y * 2 + c) * 2 + x) * 24
                block = jnp.concatenate([product[r : r + 24, :half], product[r : r + 24, half:]], 0)
                at = {"x": x, "y": y}
                g[c, at[axes[0]], at[axes[1]], z] = block.astype(BF16)


def put_chunk(product, y, axes, g):
    for c in range(2):
        for x in range(2):
            r = (c * 2 + x) * 96
            at = {"x": x, "y": y}
            g[c, at[axes[0]], at[axes[1]]] = product[r : r + 96].astype(BF16)


R = 256
FLOW_REFS = 6


def mlp_kernel(reduce, chunks, *refs):
    o, x, keep, cot, w_out, b_out, gain, bias, w1, b1, w2, b2 = refs[:12]
    mixed, dx1, do, delta, small, g_out, out1, out2 = refs[12:20]
    v1, v2, x1s, n2s, n2t, dms, gs, dus, macc, nacc, load1, load2 = refs[20:32]
    flow_refs = refs[32:]
    das = gs
    owner = lax.broadcasted_iota(jnp.int32, (16, o.shape[1]), 1) // HEAD
    heads = (owner == lax.broadcasted_iota(jnp.int32, (16, o.shape[1]), 0)).astype(BF16)
    rows, width = o.shape
    tiles = rows // R
    loads = []
    for k in range(chunks):
        cols = pl.ds(k * width, width)
        loads.append(
            (
                pltpu.make_async_copy(w1.at[:, cols], v1.at[k], load1.at[k]),
                pltpu.make_async_copy(w2.at[cols, :], v2.at[k], load2.at[k]),
            )
        )
        loads[k][0].start()
        loads[k][1].start()
    if reduce:
        place = Place()
        greet(place)
        per = 1 + FLOW_REFS
        flows1 = [Flow(place, "xy", *flow_refs[2 * per * k : 2 * per * k + per]) for k in range(chunks)]
        flows2 = [ChunkFlow(place, "yx", k, *flow_refs[2 * per * k + per : 2 * per * (k + 1)]) for k in range(chunks)]

    small[...] = jnp.zeros_like(small)

    @pl.loop(0, tiles)
    def _(t):
        r = pl.ds(pl.multiple_of(t * R, R), R)
        x1 = x[r, :].astype(F32) + keep[r, 0:1] * (mm(o[r, :], w_out[...]) + b_out[...])
        x1s[r, :] = x1
        hat, _ = row_norm(x1)
        n2 = (hat * gain[...] + bias[...]).astype(BF16)
        n2s[r, :] = n2
        dm = (cot[r, :].astype(F32) * keep[r, 1:2]).astype(BF16)
        dms[r, :] = dm
        small[7:8, :] += col_sum(dm.astype(F32))

    n2t[...] = n2s[...].T

    for k in range(chunks):
        loads[k][0].wait()
        loads[k][1].wait()

        @pl.loop(0, tiles)
        def _(t):
            r = pl.ds(pl.multiple_of(t * R, R), R)
            u = mm(n2s[r, :], v1[k]) + b1[:, k * width : k * width + width]
            dg = mm_nt(dms[r, :], v2[k])
            cdf = 0.5 + 0.5 * lax.erf(u * 0.7071067811865476)
            pdf = jnp.exp(u * u * -0.5) * 0.3989422804014327
            g = (u * cdf).astype(BF16)
            du = (dg * (cdf + u * pdf)).astype(BF16)
            gs[r, :] = g
            dus[r, :] = du
            small[3 + k : 4 + k, :] += col_sum(du.astype(F32))
            if k == 0:
                macc[r, :] = mm(g, v2[k])
                nacc[r, :] = mm_nt(du, v1[k])
            else:
                macc[r, :] += mm(g, v2[k])
                nacc[r, :] += mm_nt(du, v1[k])

        if reduce:
            if k >= 2:
                flows1[k - 2].third()
                flows2[k - 2].third()
            if k >= 1:
                flows1[k - 1].first()
                flows2[k - 1].first()

            @pl.loop(0, 2)
            def _(y):
                product = mm_tn(gs[:, pl.ds(pl.multiple_of(y * 384, 384), 384)], dms[...])
                put_chunk(product, y, "yx", flows2[k].g)

            flows2[k].start()

            @pl.loop(0, 4)
            def _(z):
                product = mm(n2t[pl.ds(pl.multiple_of(z * 192, 64), 192), :], dus[...])
                put_blocks(product, z, "xy", flows1[k].g)

            flows1[k].start()
            if k >= 1:
                flows1[k - 1].second()
                flows2[k - 1].second()
        else:

            @pl.loop(0, 3)
            def _(t):
                r = pl.ds(pl.multiple_of(t * 256, 256), 256)
                out2[pl.ds(pl.multiple_of(k * width + t * 256, 256), 256), :] = mm_tn(gs[:, r], dms[...]).astype(BF16)
                out1[r, k * width : k * width + width] = mm(n2t[r, :], dus[...]).astype(BF16)

    last = chunks - 1
    n2t[...] = o[...].T
    if reduce:
        flows1[last].first()
        flows2[last].first()
        flows1[last - 1].third()
        flows2[last - 1].third()

    @pl.loop(0, tiles)
    def _(t):
        r = pl.ds(pl.multiple_of(t * R, R), R)
        hat, rstd = row_norm(x1s[r, :])
        dn2 = nacc[r, :]
        dx = cot[r, :].astype(F32) + norm_back(hat, rstd, gain[...], dn2)
        dx1[r, :] = dx
        da = (dx * keep[r, 0:1]).astype(BF16)
        das[r, :] = da
        grad_o = mm_nt(da, w_out[...]).astype(BF16)
        do[r, :] = grad_o
        small[0:1, :] += col_sum(da.astype(F32))
        small[1:2, :] += col_sum(dn2 * hat)
        small[2:3, :] += col_sum(dn2)
        prod = grad_o.astype(F32) * o[r, :].astype(F32)
        high = prod.astype(BF16)
        low = (prod - high.astype(F32)).astype(BF16)
        sums = mm_nt(heads, high) + mm_nt(heads, low)
        for s in range(R // T):
            delta[t * (R // T) + s] = sums[:, s * T : s * T + T]

    if reduce:
        flows1[last].second()
        flows2[last].second()

        @pl.loop(0, 4)
        def _(z):
            product = mm(n2t[pl.ds(pl.multiple_of(z * 192, 64), 192), :], das[...])
            put_blocks(product, z, "xy", g_out)
    else:

        @pl.loop(0, 3)
        def _(t):
            r = pl.ds(pl.multiple_of(t * 256, 256), 256)
            g_out[r, :] = mm(n2t[r, :], das[...]).astype(BF16)

    @pl.loop(0, tiles)
    def _(t):
        r = pl.ds(pl.multiple_of(t * R, R), R)
        mixed[r, :] = (x1s[r, :] + keep[r, 1:2] * (macc[r, :] + b2[...])).astype(BF16)

    if reduce:
        half = width // 2

        def keep_share(k):
            total = flows1[k].last()
            out1[:, k * width : k * width + half] = total[:24]
            out1[:, k * width + half : (k + 1) * width] = total[24:]
            flows2[k].last_into(out2)

        for k in range(last):
            keep_share(k)
        flows1[last].third()
        flows2[last].third()
        keep_share(last)
        for k in range(chunks):
            flows1[k].finish()
            flows2[k].finish()


def mlp_step(reduce, o, x, keep, cot, w_out, b_out, gain, bias, w1, b1, w2, b2):
    rows, width = o.shape
    chunks = w1.shape[1] // width
    block = lambda dims, kind: jax.ShapeDtypeStruct(dims, kind)
    outs = [
        block((rows, width), BF16),
        block((rows, width), F32),
        block((rows, width), BF16),
        block((rows // T, 16, T), F32),
        block((16, width), F32),
    ]
    if reduce:
        outs += [block((2, 2, 2, 4, 48, width // 2), BF16), block((24, chunks * width), F32), block((96, width), F32)]
    else:
        outs += [block((width, width), BF16), block(w1.shape, BF16), block(w2.shape, BF16)]
    scratch = [
        pltpu.VMEM((chunks, width, width), BF16),
        pltpu.VMEM((chunks, width, width), BF16),
        pltpu.VMEM((rows, width), F32),
        pltpu.VMEM((rows, width), BF16),
        pltpu.VMEM((width, rows), BF16),
        pltpu.VMEM((rows, width), BF16),
        pltpu.VMEM((rows, width), BF16),
        pltpu.VMEM((rows, width), BF16),
        pltpu.VMEM((rows, width), F32),
        pltpu.VMEM((rows, width), F32),
        pltpu.SemaphoreType.DMA((chunks,)),
        pltpu.SemaphoreType.DMA((chunks,)),
    ]
    params = dict(vmem_limit_bytes=60 * 2**20)
    if reduce:
        for _ in range(chunks):
            scratch += [pltpu.VMEM((2, 2, 2, 4, 48, width // 2), BF16)] + flow_scratch(48, width // 2)
            scratch += [pltpu.VMEM((2, 2, 2, 96, width), BF16)] + chunk_scratch(96, width)
        params.update(collective_id=1, has_side_effects=True)
    anywhere = pl.BlockSpec(memory_space=pl.ANY)
    return pl.pallas_call(
        functools.partial(mlp_kernel, reduce, chunks),
        out_shape=outs,
        in_specs=[VM] * 8 + [anywhere, VM, anywhere, VM],
        out_specs=[VM] * 6 + ([VM] * 2 if reduce else [VM] * 2),
        scratch_shapes=scratch,
        compiler_params=pltpu.CompilerParams(**params),
        name="mlp_step",
    )(o, x, keep, cot, w_out, b_out, gain, bias, w1, b1, w2, b2)


class SumFlow:
    def __init__(self, place, parts, arrived, sems, recvs):
        self.place, self.parts, self.arrived = place, parts, arrived
        self.sems, self.recvs = sems, recvs
        self.copies = []

    def start(self, step):
        others = "cxy"
        if step > 0:
            self.copies[step - 1].wait_recv()
            self.parts[step] = self.parts[step - 1] + self.arrived[step - 1]
        if step < 3:
            self.copies.append(
                send(self.parts.at[step], self.arrived.at[step], self.sems.at[step], self.recvs.at[step],
                     self.place.partner(others[step]))
            )
        else:
            for d in (1, 2, 3):
                self.copies.append(
                    send(self.parts.at[3], self.arrived.at[2 + d], self.sems.at[2 + d], self.recvs.at[2 + d],
                         self.place.level(d))
                )

    def last(self):
        total = self.parts[3]
        for d in (1, 2, 3):
            self.copies[2 + d].wait_recv()
            total = total + self.arrived[2 + d]
        return total

    def finish(self):
        for copy in self.copies:
            copy.wait_send()


def tail_kernel(reduce, *refs):
    dqkv, x, dx1, gain, bias, w, g_out, small_in = refs[:8]
    grad_x, grad_w, grad_o, small = refs[8:12]
    n1s, n1t = refs[12:14]
    rest = refs[14:]
    rows, width = x.shape
    tiles = rows // R
    if reduce:
        place = Place()
        greet(place)
        out_flow = Flow(place, "xy", g_out, *rest[:6])
        flows = [Flow(place, ("yx", "xy", "yx")[i], *rest[6 + 7 * i : 13 + 7 * i]) for i in range(3)]
        sums = SumFlow(place, *rest[27:31])
        sum_parts = rest[27]
        out_flow.start()

    @pl.loop(0, tiles)
    def _(t):
        r = pl.ds(pl.multiple_of(t * R, R), R)
        hat, _ = row_norm(x[r, :].astype(F32))
        n1s[r, :] = (hat * gain[...] + bias[...]).astype(BF16)

    n1t[...] = n1s[...].T
    if reduce:
        for i in range(3):

            @pl.loop(0, 4)
            def _(z):
                product = mm(n1t[pl.ds(pl.multiple_of(z * 192, 64), 192), :], dqkv[:, i * width : (i + 1) * width])
                put_blocks(product, z, flows[i].axes, flows[i].g)

            flows[i].start()
            if i == 0:
                out_flow.first()
            else:
                flows[i - 1].first()
    else:

        @pl.loop(0, 3)
        def _(t):
            r = pl.ds(pl.multiple_of(t * 256, 256), 256)
            for i in range(3):
                grad_w[r, i * width : (i + 1) * width] = mm(n1t[r, :], dqkv[:, i * width : (i + 1) * width]).astype(BF16)

    small_ref = sum_parts.at[0] if reduce else small
    small_ref[...] = small_in[...]

    def rows_back(t):
        r = pl.ds(pl.multiple_of(t * R, R), R)
        hat, rstd = row_norm(x[r, :].astype(F32))
        dn1 = mm_nt(dqkv[r, :], w[...])
        grad_x[r, :] = dx1[r, :] + norm_back(hat, rstd, gain[...], dn1)
        small_ref[8:9, :] += col_sum(dn1 * hat)
        small_ref[9:10, :] += col_sum(dn1)
        small_ref[10:11, :] += col_sum(dqkv[r, :width].astype(F32))
        small_ref[11:12, :] += col_sum(dqkv[r, 2 * width :].astype(F32))

    pl.loop(0, tiles)(rows_back)
    if reduce:
        half = width // 2
        flows[2].first()
        sums.start(0)
        out_flow.second()
        sums.start(1)
        flows[0].second()
        sums.start(2)
        flows[1].second()
        out_flow.third()
        sums.start(3)
        flows[2].second()
        flows[0].third()
        flows[1].third()
        flows[2].third()
        total = out_flow.last()
        grad_o[:, :half] = total[:24]
        grad_o[:, half:] = total[24:]
        small[...] = sums.last()
        for i in range(3):
            total = flows[i].last()
            grad_w[:, i * width : i * width + half] = total[:24]
            grad_w[:, i * width + half : (i + 1) * width] = total[24:]
        for flow in (out_flow, *flows, sums):
            flow.finish()


def tail_step(reduce, dqkv, x, dx1, gain, bias, w, g_out, small):
    rows, width = x.shape
    block = lambda dims, kind: jax.ShapeDtypeStruct(dims, kind)
    outs = [block((rows, width), F32)]
    scratch = [pltpu.VMEM((rows, width), BF16), pltpu.VMEM((width, rows), BF16)]
    params = dict(vmem_limit_bytes=60 * 2**20)
    args = [dqkv, x, dx1, gain, bias, w, g_out, small]
    if reduce:
        outs += [block((24, 3 * width), F32), block((24, width), F32), block((16, width), F32)]
        scratch += flow_scratch(48, width // 2)
        for _ in range(3):
            scratch += [pltpu.VMEM((2, 2, 2, 4, 48, width // 2), BF16)] + flow_scratch(48, width // 2)
        scratch += [
            pltpu.VMEM((4, 16, width), F32),
            pltpu.VMEM((6, 16, width), F32),
            pltpu.SemaphoreType.DMA((6,)),
            pltpu.SemaphoreType.DMA((6,)),
        ]
        params.update(collective_id=2, has_side_effects=True)
    else:
        outs += [block(w.shape, BF16), block((8, 128), F32), block((16, width), F32)]
    return pl.pallas_call(
        functools.partial(tail_kernel, reduce),
        out_shape=outs,
        in_specs=[VM] * 8,
        out_specs=[VM] * 4,
        scratch_shapes=scratch,
        compiler_params=pltpu.CompilerParams(**params),
        name="tail_step",
    )(*args)


def layer_norm(values, gain_row, bias_row):
    center = values - jnp.mean(values, -1, keepdims=True)
    variance = jnp.mean(center * center, -1, keepdims=True)
    return center * lax.rsqrt(variance + ln_epsilon) * gain_row + bias_row


def halo_of(rows, halo, side):
    mine = jnp.where(side == 0, rows[rows.shape[0] - halo :], rows[:halo])
    return lax.ppermute(mine, "hd", [(0, 1), (1, 0)])


def in_pack_order(own, halo, side):
    return jnp.where(side == 0, jnp.concatenate([own, halo], 0), jnp.concatenate([halo, own], 0))


def per_device(tokens, image_ids, keep_masks, ln1_gain, ln1_bias, w_qkv, qv_bias, w_out, b_out,
               ln2_gain, ln2_bias, w_fc1, b_fc1, w_fc2, b_fc2, cotangent):
    rows, width = tokens.shape
    halo = 640
    both = ("seq", "hd")
    side = lax.axis_index("hd")
    reduce = lax.axis_size("seq") == 16 and lax.axis_size("hd") == 2
    halo_tiles = halo // T
    tok_halo = halo_of(tokens, halo, side)
    id_halo = halo_of(image_ids, halo, side)
    id_all = in_pack_order(image_ids, id_halo, side)
    id_tiles = id_all.reshape(-1, T)
    low = jnp.sum((id_all[None, :] < id_tiles[:, :1]).astype(jnp.int32), 1) // T
    high = (jnp.sum((id_all[None, :] <= id_tiles[:, -1:]).astype(jnp.int32), 1) + T - 1) // T
    off = jnp.where(side == 0, 0, halo_tiles).astype(jnp.int32).reshape(1)
    one_hot = (image_ids[:, None] == jnp.arange(keep_masks.shape[1], dtype=jnp.int32)[None, :]).astype(F32)
    keep_rows = jnp.dot(one_hot, keep_masks[0].astype(F32)) * drop_scale
    bias_all = jnp.concatenate([qv_bias[:width], jnp.zeros((width,), F32), qv_bias[width:]])

    def project(x):
        n = layer_norm(x.astype(F32), ln1_gain, ln1_bias).astype(BF16)
        return (mm(n, w_qkv) + bias_all).astype(BF16)

    qkv_all = in_pack_order(project(tokens), project(tok_halo), side)
    id_col, id_row = id_all[:, None], id_tiles[:, None, :]
    heads_out, lse = attn_forward(low, high, off, qkv_all, id_col, id_row, rows)
    row = lambda v: v.reshape(1, -1)
    mixed, dx1, do, delta, small, g_out, grad_fc1, grad_fc2 = mlp_step(
        reduce, heads_out, tokens, keep_rows, cotangent, w_out, row(b_out), row(ln2_gain), row(ln2_bias),
        w_fc1, row(b_fc1), w_fc2, row(b_fc2))
    stats = jnp.concatenate([lse, delta], 1)
    do_all = in_pack_order(do, halo_of(do, halo, side), side)
    stats_all = in_pack_order(stats, halo_of(stats, halo_tiles, side), side)
    dqkv = attn_backward(low, high, off, qkv_all, do_all, id_col, id_row, stats_all[:, :16], stats_all[:, 16:], rows)
    grad_x, grad_qkv, grad_out, small = tail_step(
        reduce, dqkv, tokens, dx1, row(ln1_gain), row(ln1_bias), w_qkv, g_out, small)
    if not reduce:
        grad_out = g_out

        def scatter(v):
            return lax.psum_scatter(v, both, scatter_dimension=0, tiled=True).astype(F32)

        grad_fc1, grad_fc2, grad_qkv, grad_out = map(scatter, (grad_fc1, grad_fc2, grad_qkv, grad_out))
        small = lax.psum(small, both)
    small = small.reshape(-1)
    shards = lax.axis_size("seq") * lax.axis_size("hd")
    place = lax.axis_index("seq") * lax.axis_size("hd") + side

    def share(first, count):
        part = small[first * width : (first + count) * width]
        size = count * width // shards
        return lax.dynamic_slice(part, (place * size,), (size,))

    return (mixed, grad_x, share(8, 1), share(9, 1), grad_qkv, share(10, 2), grad_out, share(0, 1),
            share(1, 1), share(2, 1), grad_fc1, share(3, 4), grad_fc2, share(7, 1))


def solution(mesh):
    both = P(("seq", "hd"))
    split = P(("seq", "hd"), None)
    return jax.shard_map(
        per_device,
        mesh=mesh,
        in_specs=(split, both, P("seq", None, None)) + (P(),) * 12 + (split,),
        out_specs=(split, split, both, both, split, both, split, both, both, both, split, both, split, both),
        check_vma=False,
    )
```

time: 1060 us -> 318 us (0.30)
  waiting for transfers between devices: 351 us -> 29.6 us
  matrix products: 297 us -> 8.41 us
  Pallas kernels: 0 us -> 235 us
  local copies, waits for them, and re-layouts: 148 us -> 24.6 us
  other arithmetic: 116 us -> 14.5 us
  blocking collectives: 96.6 us -> 0 us
  starting transfers between devices: 19.8 us -> 5.24 us
  between operations: 14.5 us -> 0.97 us
    reduce_scatter x4 -> x0, waiting for transfers between devices: 290 us -> none  [the longest x1 142 us: per_device(): lax.psum_scatter(grad_w_fc2, ('seq', 'hd'), scatter_dimension=0, tiled=True)]
    dot_general x34 -> x3, matrix products: 297 us -> 8.41 us  [the longest x2 7.37 us: mm(): return jnp.dot(a, b, preferred_element_type=F32)]
    pallas_call x0 -> x4, Pallas kernels: none -> 235 us  [the longest x1 76.8 us: mlp_step(): pl.pallas_call(functools.partial(mlp_kernel, reduce, chunks), out_shape=o...]
    convert_element_type x5 -> x0, other arithmetic: 63.5 us -> none  [the longest x3 51.5 us: one_block(): grad_low = grad_scores.astype(jnp.bfloat16)]
    all_to_all x4 -> x0, waiting for transfers between devices: 61.1 us -> none  [the longest x1 39.6 us: per_device(): lax.all_to_all(projected.reshape(tok_rows, 3, pair_count, head_width), 'h...]
    all_to_all x1 -> x0, blocking collectives: 55.3 us -> none  [per_device(): lax.all_to_all(stacked.reshape(group_rows, 3, 1, head_width), 'hd', split...]
    unnamed x1 -> x0, blocking collectives: 41.3 us -> none
    reduce_sum x9 -> x1, other arithmetic: 30.1 us -> 0.21 us  [per_device(): jnp.sum((id_all[None, :] <= id_tiles[:, -1:]).astype(jnp.int32), 1) + T - 1]
  transfers between devices with their start and end apart: 8 -> 4, of which waited for: 6 -> 2; matrix products, arithmetic and copies ran while one was open for 34% -> 5% of each run, Pallas kernels for 0% -> 0%
where the time goes in v1:
time: 318 us; the launch traced here: 319 us
  Pallas kernels  235 us (74%)
  waiting for transfers between devices  29.6 us (9%)
  local copies, waits for them, and re-layouts  24.6 us (8%)
  other arithmetic  14.5 us (5%)
  matrix products  8.41 us (3%)
  starting transfers between devices  5.24 us (2%)
    pallas_call x1, Pallas kernels, mlp_step(): pl.pallas_call(functools.partial(mlp_kernel, reduce, chunks), out_shape=o...  76.8 us
    pallas_call x1, Pallas kernels, attn_backward(): pl.pallas_call(functools.partial(attn_backward_kernel, width, tiles), out...  66.1 us
    pallas_call x1, Pallas kernels, tail_step(): pl.pallas_call(functools.partial(tail_kernel, reduce), out_shape=outs, in...  64.1 us
    ppermute x4, waiting for transfers between devices, halo_of(): return lax.ppermute(mine, 'hd', [(0, 1), (1, 0)])  29.6 us
    pallas_call x1, Pallas kernels, attn_forward(): pl.pallas_call(functools.partial(attn_forward_kernel, width, tiles), out_...  28.3 us
    dynamic_slice x8, local copies, waits for them, and re-layouts, share(): return lax.dynamic_slice(part, (place * size,), (size,))  8.75 us
    dot_general x2, matrix products, mm(): return jnp.dot(a, b, preferred_element_type=F32)  7.37 us
    select_n x5, other arithmetic, in_pack_order(): jnp.where(side == 0, jnp.concatenate([own, halo], 0), jnp.concatenate([ha...  7.23 us
  transfers between devices with their start and end apart: 4, of which 2 were waited for; matrix products, arithmetic and copies ran while one was open for 5% of the time, Pallas kernels for 0%

profile of v1, /device:TPU:0, one launch (start us, length us, event | category | flops | bytes accessed | tf_op | source)
XLA Modules:
  0.0 318.7 jit_solution(7992345765582358889)
XLA Ops:
  0.7 0.8 slice_select_fusion.3
  1.5 3.0 collective-permute-start
  4.5 2.6 slice_select_fusion.1
  7.5 0.5 fusion.2
  8.1 4.7 %add_convert_fusion = bf16[768,2304]{1,0:T(8,128)(2,1)} fusion(bf16[768,2304]{1,0:T(8,128)(2,1)S(1)} %copy-done.2, f32[2304]{0:T(1024)S(1)} %pad_maximum_fusion, bf16[768,768]{1,0:T(8,128)(2,1)S(1)} %copy-done, f32[768]{0:T(1024)S(1)} %copy-done.20, f32[768]{0:T(1024)S(1)} %copy-done.19, f32[768]{0:T(1024)S(1)} %add_rsqrt_fusion.1, ...), kind=kOutput, calls=%fused_computation | convolution fusion | flops 2724986880 | bytes 8279040 | tf_op jit(solution)/shard_map/dot_general | solution.py:18
  12.8 1.0 convolution_multiply_fusion.refs_2_
  13.9 0.6 reshape.201.refs_5_
  14.4 0.6 reshape.202.refs_6_
  15.0 0.6 reshape.203.refs_7_
  15.6 0.6 reshape.205.refs_11_
  16.8 0.6 select_n.129.id_row
  17.8 0.5 and_select_fusion
  18.4 1.0 broadcast_select_fusion.id_col
  19.3 11.2 %collective-permute-done.1 = bf16[640,768]{1,0:T(8,128)(2,1)S(1)} collective-permute-done((bf16[640,768]{1,0:T(8,128)(2,1)}, bf16[640,768]{1,0:T(8,128)(2,1)S(1)}, u32[]{:S(2)}, u32[]{:S(2)}) %collective-permute-start.1) | collective-permute-done | bytes 983072 | tf_op jit(solution)/shard_map/ppermute | solution.py:822
  30.8 0.4 fusion.8
  31.2 2.7 add_convert_fusion.1
  33.9 4.0 %maximum_select_fusion.qkv = bf16[1408,2304]{1,0:T(8,128)(2,1)} fusion(bf16[640,2304]{1,0:T(8,128)(2,1)S(1)} %add_convert_fusion.1, bf16[768,2304]{1,0:T(8,128)(2,1)S(1)} %copy-done.4, pred[]{:T(512)S(6)} %eq.8), kind=kLoop, calls=%fused_computation.1 | loop fusion | flops 29196288 | bytes 12976129 | tf_op jit(solution)/shard_map/jit(_where)/select_n | solution.py:826
  37.9 28.3 %attention_forward.1 = (bf16[768,768]{1,0:T(8,128)(2,1)}, f32[6,16,128]{2,1,0:T(8,128)}) custom-call(s32[11]{0:T(128)} %get-tuple-element.59.low_ref, s32[11]{0:T(128)} %get-tuple-element.58.high_ref, s32[1]{0:T(128)} %bitcast.1.off_ref, bf16[1408,2304]{1,0:T(8,128)(2,1)} %maximum_select_fusion.qkv, s32[1408,1]{1,0:T(8,128)} %broadcast_select_fusion.id_col, ...), custom_call_target="tpu_custom_call" | custom-call | tf_op jit(solution)/shard_map/attention_forward/pallas_call | solution.py:103
  66.2 76.8 %mlp_step.1 = (bf16[768,768]{1,0:T(8,128)(2,1)}, f32[768,768]{1,0:T(8,128)}, bf16[768,768]{1,0:T(8,128)(2,1)}, f32[6,16,128]{2,1,0:T(8,128)}, f32[16,768]{1,0:T(...) custom-call(bf16[768,768]{1,0:T(8,128)(2,1)} %get-tuple-element.28.refs_0_, ...), custom_call_target="tpu_custom_call" | custom-call | tf_op jit(solution)/shard_map/mlp_step/pallas_call | solution.py:651
  143.1 1.7 slice_select_fusion
  144.8 1.8 collective-permute-start.2
  146.6 0.4 collective-permute-start.3
  147.0 0.6 broadcast_in_dim.7.refs_3_
  147.6 0.6 broadcast_in_dim.8.refs_4_
  148.1 18.4 %collective-permute-done.3 = f32[5,32,128]{2,1,0:T(8,128)S(1)} collective-permute-done((f32[5,32,128]{2,1,0:T(8,128)S(1)}, f32[5,32,128]{2,1,0:T(8,128)S(1)}, u32[]{:S(2)}, u32[]{:S(2)}) %collective-permute-start.3) | collective-permute-done | bytes 81952 | tf_op jit(solution)/shard_map/ppermute | solution.py:822
  166.5 0.7 fusion.31
  167.2 2.2 maximum_select_fusion.1.do
  169.4 66.1 %attention_backward.1.refs_0_ = bf16[768,2304]{1,0:T(8,128)(2,1)} custom-call(s32[11]{0:T(128)} %get-tuple-element.59.low_ref, s32[11]{0:T(128)} %get-tuple-element.58.high_ref, s32[1]{0:T(128)} %bitcast.1.off_ref, bf16[1408,2304]{1,0:T(8,128)(2,1)} %maximum_select_fusion.qkv, bf16[1408,768]{1,0:T(8,128)(2,1)} %maximum_select_fusion.1.do, ...), custom_call_target="tpu_custom_call" | custom-call | tf_op jit(solution)/shard_map/attention_backward/pallas_call | solution.py:181
  235.6 64.1 %tail_step.1 = (f32[768,768]{1,0:T(8,128)}, f32[24,2304]{1,0:T(8,128)}, f32[24,768]{1,0:T(8,128)}, f32[16,768]{1,0:T(8,128)}) custom-call(bf16[768,2304]{1,0:T(8,128)(2,1)} %attention_backward.1.refs_0_, bf16[768,768]{1,0:T(8,128)(2,1)} %refs_1_.3, f32[768,768]{1,0:T(8,128)} %get-tuple-element.33.refs_2_, f32[1,768]{1,0:T(1,128)} %broadcast_in_dim.7.refs_3_, ...), custom_call_target="tpu_custom_call" | custom-call | tf_op jit(solution)/shard_map/tail_step/pallas_call | solution.py:803
  299.7 0.9 slice.99
  300.6 1.5 fusion.32
  302.1 1.3 slice.94
  303.5 0.6 slice.100
  304.1 1.3 fusion.25
  305.3 1.3 fusion.26
  306.6 1.3 fusion.27
  307.9 1.3 fusion.28
  309.1 1.3 fusion.29
  310.4 0.6 fusion.30
  311.0 0.7 slice.95
  311.7 1.3 dynamic_slice.47
  312.9 0.6 dynamic_slice.40
  313.5 1.0 copy.59
  314.6 1.4 copy.60
  316.0 0.7 copy.61
  316.7 0.6 copy.62
  317.3 0.7 copy.63
  318.0 0.7 copy.64
  (68 shorter events, 1.7 us)
Async XLA Ops:
  0.6 6.6 %copy-start = (bf16[768,768]{1,0:T(8,128)(2,1)S(1)}, bf16[768,768]{1,0:T(8,128)(2,1)}, u32[]{:S(2)}) copy-start(bf16[768,768]{1,0:T(8,128)(2,1)} %refs_1_.3) | copy-start | bytes 3538948
  0.7 6.8 %copy-start.14 = (f32[1536]{0:T(1024)S(1)}, f32[1536]{0:T(1024)}, u32[]{:S(2)}) copy-start(f32[1536]{0:T(1024)} %param.22) | copy-start | bytes 18436
  1.5 6.5 %copy-start.2 = (bf16[768,2304]{1,0:T(8,128)(2,1)S(1)}, bf16[768,2304]{1,0:T(8,128)(2,1)}, u32[]{:S(2)}) copy-start(bf16[768,2304]{1,0:T(8,128)(2,1)} %refs_5_.1) | copy-start | bytes 10616836
  1.5 6.5 %copy-start.19 = (f32[768]{0:T(1024)S(1)}, f32[768]{0:T(1024)}, u32[]{:S(2)}) copy-start(f32[768]{0:T(1024)} %param.19) | copy-start | bytes 9220
  1.5 6.6 %copy-start.20 = (f32[768]{0:T(1024)S(1)}, f32[768]{0:T(1024)}, u32[]{:S(2)}) copy-start(f32[768]{0:T(1024)} %param.20) | copy-start | bytes 9220
  1.5 14.7 %collective-permute-start = (s32[640]{0:T(1024)S(1)}, s32[640]{0:T(1024)S(1)}, u32[]{:S(2)}, u32[]{:S(2)}) collective-permute-start(s32[640]{0:T(1024)S(1)} %slice_select_fusion.3), channel_id=1, source_target_pairs={{0,1},{1,0},{2,3},{3,2},{4,5},{5,4},{6,7},{7,6},{8,9},{9,8},{10,11... | collective-permute-start | bytes 7688 | tf_op jit(solution)/shard_map/ppermute | solution.py:822
  7.1 23.4 %collective-permute-start.1 = (bf16[640,768]{1,0:T(8,128)(2,1)}, bf16[640,768]{1,0:T(8,128)(2,1)S(1)}, u32[]{:S(2)}, u32[]{:S(2)}) collective-permute-start(bf16[640,768]{1,0:T(8,128)(2,1)} %slice_select_fusion.1), channel_id=1, source_target_pairs={{0,1},{1,0},{2,3},{3,2},{4,5},{5,4},{6,7},{7,6},{8,9},{9,8},{10,11... | collective-permute-start | bytes 2949128 | tf_op jit(solution)/shard_map/ppermute | solution.py:822
  8.0 4.8 %copy-start.10 = (s32[768]{0:T(1024)S(1)}, s32[768]{0:T(1024)}, u32[]{:S(2)}) copy-start(s32[768]{0:T(1024)} %param.17) | copy-start | bytes 9220
  8.0 4.8 %copy-start.21 = (s32[1,12,2]{1,2,0:T(2,128)S(1)}, s32[1,12,2]{1,2,0:T(2,128)}, u32[]{:S(2)}) copy-start(s32[1,12,2]{1,2,0:T(2,128)} %param.18) | copy-start | bytes 292
  8.1 5.8 %copy-start.15 = (f32[768]{0:T(1024)S(1)}, f32[768]{0:T(1024)}, u32[]{:S(2)}) copy-start(f32[768]{0:T(1024)} %param.24) | copy-start | bytes 9220
  8.1 6.4 %copy-start.16 = (f32[768]{0:T(1024)S(1)}, f32[768]{0:T(1024)}, u32[]{:S(2)}) copy-start(f32[768]{0:T(1024)} %param.25) | copy-start | bytes 9220
  8.1 6.9 %copy-start.17 = (f32[768]{0:T(1024)S(1)}, f32[768]{0:T(1024)}, u32[]{:S(2)}) copy-start(f32[768]{0:T(1024)} %param.26) | copy-start | bytes 9220
  8.1 7.5 %copy-start.18 = (f32[768]{0:T(1024)S(1)}, f32[768]{0:T(1024)}, u32[]{:S(2)}) copy-start(f32[768]{0:T(1024)} %param.30) | copy-start | bytes 9220
  17.4 13.8 %copy-start.3 = (bf16[768,2304]{1,0:T(8,128)(2,1)S(1)}, bf16[768,2304]{1,0:T(8,128)(2,1)}, u32[]{:S(2)}) copy-start(bf16[768,2304]{1,0:T(8,128)(2,1)} %refs_5_.1) | copy-start | bytes 10616836
  31.2 2.7 copy-start.4
  143.0 3.5 %copy-start.13 = (f32[6,16,128]{2,1,0:T(8,128)S(1)}, f32[6,16,128]{2,1,0:T(8,128)}, u32[]{:S(2)}) copy-start(f32[6,16,128]{2,1,0:T(8,128)} %get-tuple-element.31) | copy-start | bytes 147460
  143.1 3.5 %copy-start.12 = (f32[6,16,128]{2,1,0:T(8,128)S(1)}, f32[6,16,128]{2,1,0:T(8,128)}, u32[]{:S(2)}) copy-start(f32[6,16,128]{2,1,0:T(8,128)} %get-tuple-element.32) | copy-start | bytes 147460
  143.1 24.2 %copy-start.1 = (bf16[768,768]{1,0:T(8,128)(2,1)S(1)}, bf16[768,768]{1,0:T(8,128)(2,1)}, u32[]{:S(2)}) copy-start(bf16[768,768]{1,0:T(8,128)(2,1)} %get-tuple-element.30) | copy-start | bytes 3538948
  144.8 22.4 %collective-permute-start.2 = (bf16[640,768]{1,0:T(8,128)(2,1)S(1)}, bf16[640,768]{1,0:T(8,128)(2,1)S(1)}, u32[]{:S(2)}, u32[]{:S(2)}) collective-permute-start(bf16[640,768]{1,0:T(8,128)(2,1)S(1)} %slice_select_fusion), channel_id=1, source_target_pairs={{0,1},{1,0},{2,3},{3,2},{4,5},{5,4},{6,7},{7,6},{8,9},{9,8},{10,11... | collective-permute-start | bytes 2949128 | tf_op jit(solution)/shard_map/ppermute | solution.py:822
  146.6 19.9 %collective-permute-start.3 = (f32[5,32,128]{2,1,0:T(8,128)S(1)}, f32[5,32,128]{2,1,0:T(8,128)S(1)}, u32[]{:S(2)}, u32[]{:S(2)}) collective-permute-start(f32[5,32,128]{2,1,0:T(8,128)S(1)} %slice_select_fusion.2), channel_id=1, source_target_pairs={{0,1},{1,0},{2,3},{3,2},{4,5},{5,4},{6,7},{7,6},{8,9},{9,8},{10,11... | collective-permute-start | bytes 245768 | tf_op jit(solution)/shard_map/ppermute | solution.py:822
  235.6 78.0 %copy-start.6 = (bf16[768,768]{1,0:T(8,128)(2,1)S(1)}, bf16[768,768]{1,0:T(8,128)(2,1)}, u32[]{:S(2)}) copy-start(bf16[768,768]{1,0:T(8,128)(2,1)} %get-tuple-element.74) | copy-start | bytes 3538948
  299.7 14.8 %copy-start.5 = (f32[768,768]{1,0:T(8,128)S(1)}, f32[768,768]{1,0:T(8,128)}, u32[]{:S(2)}) copy-start(f32[768,768]{1,0:T(8,128)} %get-tuple-element.75) | copy-start | bytes 7077892
  314.5 1.4 copy-start.9
  314.6 2.1 copy-start.11
  314.6 2.7 copy-start.8
  314.6 3.5 %copy-start.7 = (f32[96,768]{1,0:T(8,128)S(1)}, f32[96,768]{1,0:T(8,128)}, u32[]{:S(2)}) copy-start(f32[96,768]{1,0:T(8,128)} %get-tuple-element.86) | copy-start | bytes 884740
